TPU v7x, 32 devices: a whole 2x2x4 slice. The times are simulated.
32 devices in a mesh: groups: 1, dp: 16 (over z, y, x), tensor: 2 (over core).
Axes of the slice: x: 2, y: 2, z: 4, core: 2. Of those that a mesh axis runs over, the one named last changes fastest.
Arguments:
- inputs: bfloat16 [64, 4096], P(('groups', 'dp', 'tensor')), may hold values from -6 to 6
- out_grad: bfloat16 [64, 4096], P(('groups', 'dp', 'tensor')), may hold values from -0.8984375 to 0.8984375
- block_ids: int32 [64], P('groups'), may hold values from 0 to 15, never falling along the last dimension, each value on 1 to 8 neighbouring positions
- up_weight: bfloat16 [4096, 32768], P(None, ('dp', 'tensor')), may hold values from -0.09375 to 0.09375
- down_weight: bfloat16 [32768, 4096], P(('dp', 'tensor')), may hold values from -0.03125 to 0.03125
Outputs:
- input_grad: bfloat16 [64, 4096], P(('groups', 'dp', 'tensor'))
- neuron_scores: float32 [16, 32768], P('groups', ('dp', 'tensor'))
- up_grad: bfloat16 [4096, 32768], P('groups', ('dp', 'tensor'))
- down_grad: bfloat16 [32768, 4096], P(('groups', 'dp', 'tensor'))
Inputs may be any that keep to these rules, and one draw needn't show every extreme that they name: `block_ids`: ids never fall along the tokens; each of the 16 samples holds 1 to 8 tokens, and one holds exactly 8.
All inputs are finite; a program needn't handle non-finite values.
Results may differ from a plain program's by a relative error of at most 0.0051.
Values may be sent and summed in bfloat16 or wider, within the bound.
A program may use at most 384 MiB of HBM per device.

v0:
```python
import jax
import jax.numpy as jnp
from jax import lax
from jax.sharding import PartitionSpec as P

NBLK = 16
AXES = ("dp", "tensor")


def contract_rows(left, right):
    return lax.dot_general(
        left, right, (((0,), (0,)), ((), ())), preferred_element_type=jnp.float32
    )


def on_device(inputs, out_grad, block_ids, up_weight, down_weight):
    x_rows = lax.all_gather(inputs, AXES, axis=0, tiled=True)
    g_rows = lax.all_gather(out_grad, AXES, axis=0, tiled=True)
    block_onehot = (block_ids[:, None] == jnp.arange(NBLK, dtype=jnp.int32)[None, :]).astype(
        jnp.float32
    )
    pre = jnp.dot(x_rows, up_weight, preferred_element_type=jnp.float32)
    positive = jnp.maximum(pre, 0.0)
    act32 = positive * positive
    act_grad = lax.dot_general(
        g_rows, down_weight, (((1,), (1,)), ((), ())), preferred_element_type=jnp.float32
    )
    pre_grad = (2.0 * positive * act_grad).astype(jnp.bfloat16)
    sums = lax.dot_general(
        block_onehot,
        act32 * act_grad,
        (((0,), (0,)), ((), ())),
        precision=lax.Precision.HIGHEST,
        preferred_element_type=jnp.float32,
    )
    input_grad = lax.psum_scatter(
        lax.dot_general(
            pre_grad, up_weight, (((1,), (1,)), ((), ())), preferred_element_type=jnp.float32
        ),
        AXES,
        scatter_dimension=0,
        tiled=True,
    ).astype(jnp.bfloat16)
    return (
        input_grad,
        jnp.abs(sums),
        contract_rows(x_rows, pre_grad).astype(jnp.bfloat16),
        contract_rows(act32.astype(jnp.bfloat16), g_rows).astype(jnp.bfloat16),
    )


def solution(mesh):
    return jax.shard_map(
        on_device,
        mesh=mesh,
        in_specs=(
            P(("groups", "dp", "tensor"), None),
            P(("groups", "dp", "tensor"), None),
            P("groups"),
            P(None, ("dp", "tensor")),
            P(("dp", "tensor"), None),
        ),
        out_specs=(
            P(("groups", "dp", "tensor"), None),
            P("groups", ("dp", "tensor")),
            P("groups", ("dp", "tensor")),
            P(("groups", "dp", "tensor"), None),
        ),
        check_vma=False,
    )
```

profile of v0, /device:TPU:0, one launch (start us, length us, event | category | flops | bytes accessed | tf_op | source)
XLA Modules:
  0.0 175.4 jit_solution(2632440526007319980)
XLA Ops:
  0.6 44.9 %all-gather = bf16[32,2,4096]{2,1,0:T(2,128)(2,1)S(1)} all-gather(bf16[1,2,4096]{2,1,0:T(2,128)(2,1)} %bitcast.13), channel_id=1, replica_groups=mesh['groups'=1,'dp'=16,'tensor'=2] {'dp','tensor'}, dimensions={0}, use_global_device_ids=true | all-gather | bytes 540672 | tf_op jit(solution)/shard_map/all_gather | solution.py:17
  45.5 0.2 reshape.10
  45.7 0.0 copy-start
  45.7 5.0 %convolution_maximum_fusion = f32[64,1024]{1,0:T(8,128)S(1)} fusion(bf16[64,4096]{1,0:T(8,128)(2,1)S(1)} %reshape.10, bf16[4096,1024]{1,0:T(8,128)(2,1)} %param.8), kind=kOutput, calls=%fused_computation.2 | convolution fusion | flops 536936448 | bytes 9175040 | tf_op jit(solution)/shard_map/dot_general | solution.py:22
  50.7 0.0 copy-done
  50.7 38.1 %all-gather.1 = bf16[32,2,4096]{2,1,0:T(2,128)(2,1)S(1)} all-gather(bf16[1,2,4096]{2,1,0:T(2,128)(2,1)S(1)} %bitcast.14), channel_id=1, replica_groups=mesh['groups'=1,'dp'=16,'tensor'=2] {'dp','tensor'}, dimensions={0}, use_global_device_ids=true | all-gather | bytes 540672 | tf_op jit(solution)/shard_map/all_gather | solution.py:18
  88.8 0.2 reshape.12
  89.0 0.0 copy-start.1
  89.0 6.0 %multiply_convert_fusion = (bf16[64,1024]{1,0:T(8,128)(2,1)S(1)}, f32[64,1024]{1,0:T(8,128)S(1)}) fusion(f32[64,1024]{1,0:T(8,128)S(1)} %convolution_maximum_fusion, bf16[64,4096]{1,0:T(8,128)(2,1)S(1)} %reshape.12, bf16[1024,4096]{1,0:T(8,128)(2,1)} %param.9), kind=kOutput, calls=%fused_computation.5 | convolution fusion | flops 537067520 | bytes 9568256 | tf_op jit(solution)/shard_map/dot_general | solution.py:25
  95.0 6.0 %fusion.3 = f32[64,4096]{1,0:T(8,128)S(1)} fusion(bf16[64,1024]{1,0:T(8,128)(2,1)S(1)} %get-tuple-element.12, bf16[4096,1024]{1,0:T(8,128)(2,1)} %param.8), kind=kOutput, calls=%fused_computation.11 | convolution fusion | flops 536870912 | bytes 9568256 | tf_op jit(solution)/shard_map/dot_general | solution.py:37
  101.1 49.3 %all-reduce.2 = bf16[64,4096]{1,0:T(8,128)(2,1)S(1)} all-reduce(f32[64,4096]{1,0:T(8,128)S(1)} %fusion.3), channel_id=2, replica_groups=mesh['groups'=1,'dp'=16,'tensor'=2] {'dp','tensor'}, use_global_device_ids=true, to_apply=%region_0.0.clone | all-reduce | flops 262144 | bytes 1572864
  150.4 0.6 dynamic-slice_convert_fusion
  151.0 0.0 copy-done.1
  151.0 0.9 convolution_abs_fusion
  152.0 5.8 %convert_bitcast_fusion = bf16[4096,1024]{0,1:T(8,128)(2,1)} fusion(bf16[64,1024]{1,0:T(8,128)(2,1)S(1)} %get-tuple-element.12, bf16[64,4096]{1,0:T(8,128)(2,1)S(1)} %reshape.10), kind=kOutput, calls=%fused_computation | convolution fusion | flops 541065216 | bytes 9043968 | tf_op jit(solution)/shard_map/dot_general | solution.py:11
  157.7 11.9 %copy.10 = bf16[4096,1024]{1,0:T(8,128)(2,1)} copy(bf16[4096,1024]{0,1:T(8,128)(2,1)} %convert_bitcast_fusion) | data formatting | bytes 16777216
  169.7 5.8 %convolution_convert_fusion = bf16[1024,4096]{1,0:T(8,128)(2,1)} fusion(bf16[64,4096]{1,0:T(8,128)(2,1)S(1)} %reshape.12, f32[64,1024]{1,0:T(8,128)S(1)} %convolution_maximum_fusion), kind=kOutput, calls=%fused_computation.1 | convolution fusion | flops 541196288 | bytes 9175040 | tf_op jit(solution)/shard_map/dot_general | solution.py:11
Async XLA Ops:
  45.7 5.0 %copy-start = (bf16[2,4096]{1,0:T(2,128)(2,1)S(1)}, bf16[2,4096]{1,0:T(2,128)(2,1)}, u32[]{:S(2)}) copy-start(bf16[2,4096]{1,0:T(2,128)(2,1)} %param.6) | copy-start | bytes 49156
  89.0 62.1 %copy-start.1 = (s32[64]{0:T(128)S(1)}, s32[64]{0:T(128)}, u32[]{:S(2)}) copy-start(s32[64]{0:T(128)} %param.7) | copy-start | bytes 772
where the time goes:
time: 176 us; the launch traced here: 175 us
  blocking collectives  132 us (75%)
  matrix products  29.5 us (17%)
  local copies, waits for them, and re-layouts  13 us (7%)
    unnamed x1, blocking collectives  49.3 us
    all_gather x1, blocking collectives, on_device(): x_rows = lax.all_gather(inputs, AXES, axis=0, tiled=True)  44.9 us
    all_gather x1, blocking collectives, on_device(): g_rows = lax.all_gather(out_grad, AXES, axis=0, tiled=True)  38.1 us
    unnamed x7, local copies, waits for them, and re-layouts  12.3 us
    dot_general x2, matrix products, contract_rows(): lax.dot_general(left, right, (((0,), (0,)), ((), ())), preferred_element_...  11.5 us
    dot_general x1, matrix products, on_device(): lax.dot_general(g_rows, down_weight, (((1,), (1,)), ((), ())), preferred_...  6.04 us
    dot_general x1, matrix products, on_device(): lax.dot_general(pre_grad, up_weight, (((1,), (1,)), ((), ())), preferred_...  6.04 us
    dot_general x1, matrix products, on_device(): pre = jnp.dot(x_rows, up_weight, preferred_element_type=jnp.float32)  4.95 us

commit v1 on v0

v1 whole, which is shorter than its diff:
```python
import functools

import jax
import jax.numpy as jnp
from jax import lax
from jax.experimental import pallas as pl
from jax.experimental.pallas import tpu as pltpu
from jax.sharding import PartitionSpec as P

NBLK = 16
TILE = 16
MESH = pl.DeviceIdType.MESH
F32, BF16 = jnp.float32, jnp.bfloat16


def orders(count_dp):
    bits = count_dp.bit_length() - 1
    first = list(range(bits - 1, -1, -1))
    second = list(first)
    if bits >= 4:
        second[2], second[3] = second[3], second[2]
    return first, second


def position(dp, order):
    return sum(((dp // 2**b) % 2) * 2**k for k, b in enumerate(order))


def swapped(p):
    return (p & ~12) | ((p & 4) << 1) | ((p & 8) >> 1)


def permutation(group, rows, pieces, second, flip):
    size = group * TILE
    m = lax.broadcasted_iota(jnp.int32, (size, size), 1 if flip else 0)
    k = lax.broadcasted_iota(jnp.int32, (size, size), 0 if flip else 1)
    row = m & (rows - 1)
    place = (m >> (rows.bit_length() - 1)) & (group - 1)
    piece = m >> ((rows * group).bit_length() - 1)
    if second and group >= 16:
        place = swapped(place)
    return jnp.where(k == place * TILE + piece * rows + row, 1.0, 0.0).astype(BF16)


def sample_rows(ids, tokens, rows, count_dp, order):
    shape = (tokens, tokens)
    nat = lax.broadcasted_iota(jnp.int32, shape, 0)
    can = lax.broadcasted_iota(jnp.int32, shape, 1)
    shift = rows.bit_length() - 1
    place = (can >> shift) & (count_dp - 1)
    core = can >> (shift + count_dp.bit_length() - 1)
    dp = sum((((place >> k) & 1) << b for k, b in enumerate(order)), jnp.zeros_like(place))
    want = (dp * 2 + core) * rows + (can & (rows - 1))
    move = jnp.where(nat == want, 1.0, 0.0).astype(BF16)
    natural = jnp.where(
        lax.broadcasted_iota(jnp.int32, (NBLK, tokens), 0) == ids, 1.0, 0.0
    ).astype(BF16)
    return jnp.dot(natural, move, preferred_element_type=F32)


def exchange_kernel(
    count_dp, x_ref, g_ref, ids_ref, up_hbm, down_hbm,
    ig_ref, sc_ref, xa_ref, ga_ref, act_ref, pg_ref,
    upv, dnv, bufx, bufg, perm, zs, snd0, rcv0, snd, rcv, acc,
    wsem, gs, gr, cs, cr, r0s, r0r, rs, rr,
):
    rows, feats = x_ref.shape
    width = dnv.shape[0]
    tokens = xa_ref.shape[0]
    pieces = TILE // rows
    lanes = feats // pieces
    half = lanes // 2
    group = min(16, count_dp)
    groups = count_dp // group
    span = group * rows
    order = orders(count_dp)
    bits = len(order[0])
    dp = lax.axis_index("dp")
    core = lax.axis_index("tensor")
    other = 1 - core
    pos = [position(dp, o) for o in order]

    loads = []
    for i in range(4):
        a, b = feats // 4, width // 4
        loads.append(pltpu.make_async_copy(up_hbm.at[pl.ds(i * a, a)], upv.at[pl.ds(i * a, a)], wsem.at[i]))
        loads.append(pltpu.make_async_copy(down_hbm.at[pl.ds(i * b, b)], dnv.at[pl.ds(i * b, b)], wsem.at[4 + i]))
    for load in loads:
        load.start()

    def to_dp(h, bit):
        b = order[h][bit]
        side = (dp // 2**b) % 2
        return {"dp": dp + (1 - 2 * side) * 2**b}

    def remote(src, dst, s, r, device):
        copy = pltpu.make_async_remote_copy(
            src_ref=src, dst_ref=dst, send_sem=s, recv_sem=r, device_id=device, device_id_type=MESH
        )
        copy.start()
        return copy

    barrier = pltpu.get_barrier_semaphore()
    for k in range(bits):
        pl.semaphore_signal(barrier, inc=1, device_id=to_dp(0, k), device_id_type=MESH)
    pl.semaphore_signal(barrier, inc=1, device_id={"tensor": other}, device_id_type=MESH)

    bufs = (bufx, bufg)
    for h, ref in enumerate((x_ref, g_ref)):
        wide = ref[...].astype(F32)
        block = jnp.concatenate([wide[:, c * lanes:(c + 1) * lanes] for c in range(pieces)], axis=0)
        bufs[h][core, pos[h]] = block.astype(BF16)
    pl.semaphore_wait(barrier, bits + 1)

    steps = [[], []]
    shared = [[], []]

    def share(h, j, start, size):
        part = bufs[h].at[core, pl.ds(start, size)]
        shared[h].append(remote(part, part, cs.at[h, j], cr.at[h, j], {"tensor": other}))

    for k in range(bits + 1):
        for h in range(2):
            if k > 0:
                steps[h][k - 1].wait_recv()
            if k < bits:
                size = 2**k
                part = bufs[h].at[core, pl.ds((pos[h] // size) * size, size)]
                steps[h].append(remote(part, part, gs.at[h, k], gr.at[h, k], to_dp(h, k)))
            if k == 0:
                share(h, 0, pos[h], 1)
            else:
                size = 2 ** (k - 1)
                mine = pos[h] // size
                share(h, k, (mine + 1 - 2 * (mine % 2)) * size, size)
            if k == 0:
                perm[h] = permutation(group, rows, pieces, h == 1, False)
                perm[2 + h] = permutation(group, rows, pieces, h == 1, True)
    samples = sample_rows(ids_ref[...], tokens, rows, count_dp, order[0])
    for h in range(2):
        for copy in shared[h]:
            copy.wait_recv()
    for h, whole in enumerate((xa_ref, ga_ref)):
        for cc in range(2):
            for gi in range(groups):
                block = bufs[h][cc, gi * group:(gi + 1) * group].reshape(group * TILE, lanes)
                y = jnp.dot(perm[h], block, preferred_element_type=F32).astype(BF16)
                r0 = (cc * groups + gi) * span
                for c in range(pieces):
                    whole[r0:r0 + span, c * lanes:(c + 1) * lanes] = y[c * span:(c + 1) * span]
    for load in loads:
        load.wait()

    nb = min(256, width)
    for n in range(width // nb):
        cols = slice(n * nb, (n + 1) * nb)
        pre = jnp.dot(xa_ref[...], upv[:, cols], preferred_element_type=F32)
        act_grad = lax.dot_general(
            ga_ref[...], dnv[cols, :], (((1,), (1,)), ((), ())), preferred_element_type=F32
        )
        positive = jnp.maximum(pre, 0.0)
        act32 = positive * positive
        act_ref[:, cols] = act32.astype(BF16)
        pg_ref[:, cols] = (2.0 * positive * act_grad).astype(BF16)
        sc_ref[:, cols] = jnp.abs(
            jnp.dot(samples, act32 * act_grad, precision=lax.Precision.HIGHEST, preferred_element_type=F32)
        )

    for c in range(pieces):
        z = lax.dot_general(
            pg_ref[...], upv[c * lanes:(c + 1) * lanes, :], (((1,), (1,)), ((), ())),
            preferred_element_type=F32,
        ).astype(BF16)
        for cc in range(2):
            for gi in range(groups):
                r0 = (cc * groups + gi) * span
                zs[cc, gi, c * span:(c + 1) * span, :] = z[r0:r0 + span]

    def by_place(h, side, gi):
        v = jnp.dot(perm[2 + h], zs[side, gi, :, h * half:(h + 1) * half], preferred_element_type=F32)
        return v.reshape(group, TILE, half)

    pair = []
    for h in range(2):
        for gi in range(groups):
            snd0[h, gi * group:(gi + 1) * group] = by_place(h, other, gi).astype(BF16)
        pair.append(remote(snd0.at[h], rcv0.at[h], r0s.at[h], r0r.at[h], {"tensor": other}))
    for h in range(2):
        for gi in range(groups):
            acc[h, gi * group:(gi + 1) * group] = by_place(h, core, gi)
    sums = [[], []]
    for k in range(bits - 1, -1, -1):
        size = 2**k
        for h in range(2):
            side = (pos[h] // size) % 2
            base = (pos[h] // (2 * size)) * (2 * size)
            if k == bits - 1:
                pair[h].wait_recv()
                acc[h] = acc[h] + rcv0[h].astype(F32)
            else:
                sums[h][-1].wait_recv()
                now = pl.ds(base, 2 * size)
                acc[h, now] = acc[h, now] + rcv[h, 2 * size:4 * size].astype(F32)
            snd[h, size:2 * size] = acc[h, pl.ds(base + (1 - side) * size, size)].astype(BF16)
            sums[h].append(
                remote(
                    snd.at[h, pl.ds(size, size)], rcv.at[h, pl.ds(size, size)],
                    rs.at[h, k], rr.at[h, k], to_dp(h, k),
                )
            )
    last = []
    for h in range(2):
        sums[h][-1].wait_recv()
        last.append(acc[h, pos[h]] + rcv[h, 1].astype(F32))
    ig_ref[...] = jnp.concatenate(
        [last[h][c * rows:(c + 1) * rows] for c in range(pieces) for h in range(2)], axis=1
    ).astype(BF16)
    for h in range(2):
        for copy in steps[h] + shared[h] + [pair[h]] + sums[h]:
            copy.wait_send()


def weight_grads_kernel(x_ref, pg_ref, act_ref, g_ref, up_ref, down_ref):
    contract = (((0,), (0,)), ((), ()))
    up_ref[...] = lax.dot_general(x_ref[...], pg_ref[...], contract, preferred_element_type=F32).astype(BF16)
    down_ref[...] = lax.dot_general(act_ref[...], g_ref[...], contract, preferred_element_type=F32).astype(BF16)


def on_device(inputs, out_grad, block_ids, up_weight, down_weight):
    rows, feats = inputs.shape
    width = up_weight.shape[1]
    count_dp = lax.axis_size("dp")
    tokens = rows * count_dp * 2
    lanes = feats * rows // TILE
    half = lanes // 2
    group = min(16, count_dp)
    groups = count_dp // group
    bits = count_dp.bit_length() - 1
    vmem = pl.BlockSpec(memory_space=pltpu.VMEM)
    hbm = pl.BlockSpec(memory_space=pl.ANY)
    sem = pltpu.SemaphoreType.DMA
    input_grad, scores, x_all, g_all, act, pre_grad = pl.pallas_call(
        functools.partial(exchange_kernel, count_dp),
        out_shape=(
            jax.ShapeDtypeStruct((rows, feats), BF16),
            jax.ShapeDtypeStruct((NBLK, width), F32),
            jax.ShapeDtypeStruct((tokens, feats), BF16),
            jax.ShapeDtypeStruct((tokens, feats), BF16),
            jax.ShapeDtypeStruct((tokens, width), BF16),
            jax.ShapeDtypeStruct((tokens, width), BF16),
        ),
        in_specs=[vmem, vmem, vmem, hbm, hbm],
        out_specs=(vmem,) * 6,
        scratch_shapes=[
            pltpu.VMEM((feats, width), BF16),
            pltpu.VMEM((width, feats), BF16),
            pltpu.VMEM((2, count_dp, TILE, lanes), BF16),
            pltpu.VMEM((2, count_dp, TILE, lanes), BF16),
            pltpu.VMEM((4, group * TILE, group * TILE), BF16),
            pltpu.VMEM((2, groups, group * TILE, lanes), BF16),
            pltpu.VMEM((2, count_dp, TILE, half), BF16),
            pltpu.VMEM((2, count_dp, TILE, half), BF16),
            pltpu.VMEM((2, count_dp, TILE, half), BF16),
            pltpu.VMEM((2, count_dp, TILE, half), BF16),
            pltpu.VMEM((2, count_dp, TILE, half), F32),
            sem((8,)),
            sem((2, bits)), sem((2, bits)),
            sem((2, bits + 1)), sem((2, bits + 1)),
            sem((2,)), sem((2,)),
            sem((2, bits)), sem((2, bits)),
        ],
        compiler_params=pltpu.CompilerParams(
            collective_id=0, has_side_effects=True, vmem_limit_bytes=48 * 2**20
        ),
        cost_estimate=pl.CostEstimate(
            flops=6 * tokens * feats * width, bytes_accessed=4 * feats * width, transcendentals=0
        ),
        name="exchange",
    )(inputs, out_grad, block_ids.reshape(1, tokens), up_weight, down_weight)
    parts = 8
    up_grad, down_grad = pl.pallas_call(
        weight_grads_kernel,
        grid=(parts,),
        out_shape=(
            jax.ShapeDtypeStruct((feats, width), BF16),
            jax.ShapeDtypeStruct((width, feats), BF16),
        ),
        in_specs=[
            pl.BlockSpec((tokens, feats // parts), lambda i: (0, i)),
            pl.BlockSpec((tokens, width), lambda i: (0, 0)),
            pl.BlockSpec((tokens, width), lambda i: (0, 0)),
            pl.BlockSpec((tokens, feats // parts), lambda i: (0, i)),
        ],
        out_specs=(
            pl.BlockSpec((feats // parts, width), lambda i: (i, 0)),
            pl.BlockSpec((width, feats // parts), lambda i: (0, i)),
        ),
        compiler_params=pltpu.CompilerParams(vmem_limit_bytes=32 * 2**20),
        cost_estimate=pl.CostEstimate(
            flops=4 * tokens * feats * width, bytes_accessed=4 * feats * width, transcendentals=0
        ),
        name="weight_grads",
    )(x_all, pre_grad, act, g_all)
    return input_grad, scores, up_grad, down_grad


def solution(mesh):
    return jax.shard_map(
        on_device,
        mesh=mesh,
        in_specs=(
            P(("groups", "dp", "tensor"), None),
            P(("groups", "dp", "tensor"), None),
            P("groups"),
            P(None, ("dp", "tensor")),
            P(("dp", "tensor"), None),
        ),
        out_specs=(
            P(("groups", "dp", "tensor"), None),
            P("groups", ("dp", "tensor")),
            P("groups", ("dp", "tensor")),
            P(("groups", "dp", "tensor"), None),
        ),
        check_vma=False,
    )
```

time: 176 us -> 56 us (0.32)
  blocking collectives: 132 us -> 0 us
  Pallas kernels: 0 us -> 51.7 us
  matrix products: 29.5 us -> 0 us
  local copies, waits for them, and re-layouts: 13 us -> 3.32 us
    all_gather x2 -> x0, blocking collectives: 83 us -> none  [the longest x1 44.9 us: on_device(): x_rows = lax.all_gather(inputs, AXES, axis=0, tiled=True)]
    pallas_call x0 -> x2, Pallas kernels: none -> 51.7 us  [the longest x1 43.9 us: on_device(): pl.pallas_call(functools.partial(exchange_kernel, count_dp), out_shape=(j...]
    unnamed x1 -> x0, blocking collectives: 49.3 us -> none
    dot_general x6 -> x0, matrix products: 29.5 us -> none  [the longest x2 11.5 us: contract_rows(): lax.dot_general(left, right, (((0,), (0,)), ((), ())), preferred_element_...]
    unnamed x7 -> x8, local copies, waits for them, and re-layouts: 12.3 us -> 3.32 us
where the time goes in v1:
time: 56 us; the launch traced here: 55.7 us
  Pallas kernels  51.7 us (92%)
  local copies, waits for them, and re-layouts  3.32 us (6%)
  between operations  0.65 us (1%)
    pallas_call x1, Pallas kernels, on_device(): pl.pallas_call(functools.partial(exchange_kernel, count_dp), out_shape=(j...  43.9 us
    pallas_call x1, Pallas kernels, on_device(): pl.pallas_call(weight_grads_kernel, grid=(parts,), out_shape=(jax.ShapeDt...  7.84 us
    unnamed x8, local copies, waits for them, and re-layouts  3.32 us

profile of v1, /device:TPU:0, one launch (start us, length us, event | category | flops | bytes accessed | tf_op | source)
XLA Modules:
  0.0 55.7 jit_solution(614467311753589210)
XLA Ops:
  0.6 0.0 copy-start
  0.6 0.7 %copy-done = bf16[2,4096]{1,0:T(2,128)(2,1)S(1)} copy-done((bf16[2,4096]{1,0:T(2,128)(2,1)S(1)}, bf16[2,4096]{1,0:T(2,128)(2,1)}, u32[]{:S(2)}) %copy-start) | copy-done | bytes 16408
  1.4 0.0 copy-start.1
  1.4 0.7 %copy-done.1 = bf16[2,4096]{1,0:T(2,128)(2,1)S(1)} copy-done((bf16[2,4096]{1,0:T(2,128)(2,1)S(1)}, bf16[2,4096]{1,0:T(2,128)(2,1)}, u32[]{:S(2)}) %copy-start.1) | copy-done | bytes 16408
  2.1 0.0 copy-start.2
  2.1 0.7 %copy-done.2 = s32[64]{0:T(128)S(1)} copy-done((s32[64]{0:T(128)S(1)}, s32[64]{0:T(128)}, u32[]{:S(2)}) %copy-start.2) | copy-done | bytes 280
  2.7 43.9 %exchange.1 = (bf16[2,4096]{1,0:T(2,128)(2,1)S(1)}, f32[16,1024]{1,0:T(8,128)S(1)}, bf16[64,4096]{1,0:T(8,128)(2,1)S(1)}, bf16[64,4096]{1,0:T(8,128)(2,1)S(1)}, ...) custom-call(bf16[2,4096]{1,0:T(2,128)(2,1)S(1)} %copy-done, bf16[2,4096]{1,0:T(2,128)(2,1)S(1)} %copy-done.1, ...), custom_call_target="tpu_custom_call" | custom-call | flops 1610612736 | bytes 16777216 | tf_op jit(solution)/shard_map/exchange/pallas_call | solution.py:242
  46.6 7.8 %weight_grads.1 = (bf16[4096,1024]{1,0:T(8,128)(2,1)}, bf16[1024,4096]{1,0:T(8,128)(2,1)}) custom-call(bf16[64,4096]{1,0:T(8,128)(2,1)S(1)} %get-tuple-element.14.x_ref, bf16[64,1024]{1,0:T(8,128)(2,1)S(1)} %get-tuple-element.15.pg_ref, bf16[64,1024]{1,0:T(8,128)(2,1)S(1)} %get-tuple-element.16.act_ref, bf16[64,4096]{1,0:T(8,128)(2,1)S(1)} %get-tuple-element.17.g_ref), custom_call_target="tpu_custom_call" | custom-call | flops 1073741824 | bytes 16777216 | tf_op jit(solution)/shard_map/weight_grads/pallas_call | solution.py:281
  54.5 0.6 %copy.11 = bf16[2,4096]{1,0:T(2,128)(2,1)} copy(bf16[2,4096]{1,0:T(2,128)(2,1)S(1)} %get-tuple-element.24) | data formatting | bytes 32768
  55.1 0.6 %copy.12 = f32[16,1024]{1,0:T(8,128)} copy(f32[16,1024]{1,0:T(8,128)S(1)} %get-tuple-element.25) | data formatting | bytes 131072
Async XLA Ops:
  0.6 0.7 %copy-start = (bf16[2,4096]{1,0:T(2,128)(2,1)S(1)}, bf16[2,4096]{1,0:T(2,128)(2,1)}, u32[]{:S(2)}) copy-start(bf16[2,4096]{1,0:T(2,128)(2,1)} %x_ref.1) | copy-start | bytes 49156
  1.4 0.7 %copy-start.1 = (bf16[2,4096]{1,0:T(2,128)(2,1)S(1)}, bf16[2,4096]{1,0:T(2,128)(2,1)}, u32[]{:S(2)}) copy-start(bf16[2,4096]{1,0:T(2,128)(2,1)} %g_ref.1) | copy-start | bytes 49156
  2.1 0.7 %copy-start.2 = (s32[64]{0:T(128)S(1)}, s32[64]{0:T(128)}, u32[]{:S(2)}) copy-start(s32[64]{0:T(128)} %param.7) | copy-start | bytes 772

commit v2 on v1

v2 whole, which is shorter than its diff:
```python
import functools

import jax
import jax.numpy as jnp
from jax import lax
from jax.experimental import pallas as pl
from jax.experimental.pallas import tpu as pltpu
from jax.sharding import PartitionSpec as P

NBLK = 16
TILE = 16
MESH = pl.DeviceIdType.MESH
F32, BF16 = jnp.float32, jnp.bfloat16


def permutation(group, rows, flip):
    size = group * TILE
    m = lax.broadcasted_iota(jnp.int32, (size, size), 1 if flip else 0)
    k = lax.broadcasted_iota(jnp.int32, (size, size), 0 if flip else 1)
    row = m & (rows - 1)
    place = (m >> (rows.bit_length() - 1)) & (group - 1)
    piece = m >> ((rows * group).bit_length() - 1)
    return jnp.where(k == place * TILE + piece * rows + row, 1.0, 0.0).astype(BF16)


def sample_rows(ids, tokens, rows, count_dp):
    nat = lax.broadcasted_iota(jnp.int32, (tokens, tokens), 0)
    can = lax.broadcasted_iota(jnp.int32, (tokens, tokens), 1)
    shift = rows.bit_length() - 1
    dp = (can >> shift) & (count_dp - 1)
    core = can >> (shift + count_dp.bit_length() - 1)
    want = (dp * 2 + core) * rows + (can & (rows - 1))
    move = jnp.where(nat == want, 1.0, 0.0).astype(BF16)
    natural = jnp.where(
        lax.broadcasted_iota(jnp.int32, (NBLK, tokens), 0) == ids, 1.0, 0.0
    ).astype(BF16)
    return jnp.dot(natural, move, preferred_element_type=F32)


def exchange_kernel(
    count_dp, near, xg_ref, up_hbm, down_hbm,
    ig_ref, prod_ref, xa_ref, ga_ref, act_ref, pg_ref,
    upv, dnv, buf, perm, zs, snd0, rcv0, acc, snd1, rcv1, snd2, rcv2,
    wsem, hs, hr, ls, lr, cs, cr, p0s, p0r, p1s, p1r, p2s, p2r,
):
    rows, feats = ig_ref.shape
    width = dnv.shape[0]
    pieces = TILE // rows
    lanes = feats // pieces
    group = min(16, count_dp)
    groups = count_dp // group
    span = group * rows
    far = count_dp // near
    dp = lax.axis_index("dp")
    core = lax.axis_index("tensor")
    other = 1 - core
    hi, lo = dp // near, dp % near
    steps = sorted(range(1, far), key=lambda j: (min(j, far - j), j))

    loads = []
    for i in range(4):
        a, b = feats // 4, width // 4
        loads.append(pltpu.make_async_copy(up_hbm.at[pl.ds(i * a, a)], upv.at[pl.ds(i * a, a)], wsem.at[i]))
        loads.append(pltpu.make_async_copy(down_hbm.at[pl.ds(i * b, b)], dnv.at[pl.ds(i * b, b)], wsem.at[4 + i]))
    for load in loads:
        load.start()

    def far_peer(j):
        return {"dp": (hi + j) % far * near + lo}

    def near_peer(j):
        return {"dp": hi * near + (lo + j) % near}

    sent = []

    def remote(src, dst, s, r, device):
        copy = pltpu.make_async_remote_copy(
            src_ref=src, dst_ref=dst, send_sem=s, recv_sem=r, device_id=device, device_id_type=MESH
        )
        copy.start()
        sent.append(copy)
        return copy

    barrier = pltpu.get_barrier_semaphore()
    peers = [far_peer(j) for j in range(1, far)] + [near_peer(j) for j in range(1, near)]
    for peer in peers + [{"tensor": other}]:
        pl.semaphore_signal(barrier, inc=1, device_id=peer, device_id_type=MESH)
    wide = xg_ref[...].astype(F32)
    for h in range(2):
        block = jnp.concatenate(
            [wide[h * rows:(h + 1) * rows, c * lanes:(c + 1) * lanes] for c in range(pieces)], axis=0
        )
        buf[core, dp, h] = block.astype(BF16)
    pl.semaphore_wait(barrier, len(peers) + 1)

    own = buf.at[core, dp]
    over_far = {j: remote(own, own, hs.at[j - 1], hr.at[j - 1], far_peer(j)) for j in steps}
    over_near, shared = {}, []

    def pass_on(j, place):
        part = buf.at[core, place]
        for i in range(1, near):
            over_near[j, i] = remote(part, part, ls.at[j, i - 1], lr.at[j, i - 1], near_peer(i))
        share(j, 0, place)

    def share(j, i, place):
        part = buf.at[core, place]
        shared.append(remote(part, part, cs.at[j, i], cr.at[j, i], {"tensor": other}))

    pass_on(0, dp)
    perm[0] = permutation(group, rows, False)
    perm[1] = permutation(group, rows, True)
    for j in steps:
        over_far[j].wait_recv()
        pass_on(j, (hi + far - j) % far * near + lo)
    for j in [0] + steps:
        for i in range(1, near):
            over_near[j, i].wait_recv()
            share(j, i, (hi + far - j) % far * near + (lo + near - i) % near)
    for copy in shared:
        copy.wait_recv()

    for h, whole in enumerate((xa_ref, ga_ref)):
        for cc in range(2):
            for gi in range(groups):
                block = buf[cc, gi * group:(gi + 1) * group, h].reshape(group * TILE, lanes)
                y = jnp.dot(perm[0], block, preferred_element_type=F32).astype(BF16)
                r0 = (cc * groups + gi) * span
                for c in range(pieces):
                    whole[r0:r0 + span, c * lanes:(c + 1) * lanes] = y[c * span:(c + 1) * span]
    for load in loads:
        load.wait()

    nb = min(256, width)
    for n in range(width // nb):
        cols = slice(n * nb, (n + 1) * nb)
        pre = jnp.dot(xa_ref[...], upv[:, cols], preferred_element_type=F32)
        act_grad = lax.dot_general(
            ga_ref[...], dnv[cols, :], (((1,), (1,)), ((), ())), preferred_element_type=F32
        )
        positive = jnp.maximum(pre, 0.0)
        act32 = positive * positive
        act_ref[:, cols] = act32.astype(BF16)
        pg_ref[:, cols] = (2.0 * positive * act_grad).astype(BF16)
        prod_ref[:, cols] = act32 * act_grad

    for c in range(pieces):
        z = lax.dot_general(
            pg_ref[...], upv[c * lanes:(c + 1) * lanes, :], (((1,), (1,)), ((), ())),
            preferred_element_type=F32,
        ).astype(BF16)
        for cc in range(2):
            for gi in range(groups):
                r0 = (cc * groups + gi) * span
                zs[cc, gi, c * span:(c + 1) * span, :] = z[r0:r0 + span]

    def by_place(side, gi):
        v = jnp.dot(perm[1], zs[side, gi], preferred_element_type=F32)
        return v.reshape(group, TILE, lanes)

    for gi in range(groups):
        snd0[gi * group:(gi + 1) * group] = by_place(other, gi).astype(BF16)
    order = steps[::-1] + [0]
    pair = {}
    for j in order:
        block = pl.ds((hi + j) % far * near, near)
        pair[j] = remote(snd0.at[block], rcv0.at[block], p0s.at[j], p0r.at[j], {"tensor": other})
    for gi in range(groups):
        acc[gi * group:(gi + 1) * group] = by_place(core, gi)
    to_near, to_far = {}, {}
    for j in order:
        start = (hi + j) % far * near
        block = pl.ds(start, near)
        pair[j].wait_recv()
        both = acc[block] + rcv0[block].astype(F32)
        acc[block] = both
        snd1[block] = both.astype(BF16)
        for i in range(1, near):
            to_near[j, i] = remote(
                snd1.at[start + (lo + i) % near], rcv1.at[j, i - 1],
                p1s.at[j, i - 1], p1r.at[j, i - 1], near_peer(i),
            )
    total = None
    for j in order:
        total = acc[(hi + j) % far * near + lo]
        for i in range(1, near):
            to_near[j, i].wait_recv()
            total = total + rcv1[j, i - 1].astype(F32)
        if j > 0:
            snd2[j - 1] = total.astype(BF16)
            to_far[j] = remote(snd2.at[j - 1], rcv2.at[j - 1], p2s.at[j - 1], p2r.at[j - 1], far_peer(j))
    for j in order[:-1]:
        to_far[j].wait_recv()
        total = total + rcv2[j - 1].astype(F32)
    ig_ref[...] = jnp.concatenate([total[c * rows:(c + 1) * rows] for c in range(pieces)], axis=1)
    for copy in sent:
        copy.wait_send()


def weight_grads_kernel(
    count_dp, sum_ref, prod_ref, ids_ref, x_ref, pg_ref, act_ref, g_ref,
    ig_ref, sc_ref, up_ref, down_ref,
):
    @pl.when(pl.program_id(0) == 0)
    def _():
        rows, tokens = ig_ref.shape[0], ids_ref.shape[1]
        ig_ref[...] = sum_ref[...].astype(BF16)
        samples = sample_rows(ids_ref[...], tokens, rows, count_dp)
        sc_ref[...] = jnp.abs(
            jnp.dot(samples, prod_ref[...], precision=lax.Precision.HIGHEST, preferred_element_type=F32)
        )

    contract = (((0,), (0,)), ((), ()))
    up_ref[...] = lax.dot_general(x_ref[...], pg_ref[...], contract, preferred_element_type=F32).astype(BF16)
    down_ref[...] = lax.dot_general(act_ref[...], g_ref[...], contract, preferred_element_type=F32).astype(BF16)


def on_device(inputs, out_grad, block_ids, up_weight, down_weight):
    rows, feats = inputs.shape
    width = up_weight.shape[1]
    count_dp = lax.axis_size("dp")
    tokens = rows * count_dp * 2
    lanes = feats * rows // TILE
    group = min(16, count_dp)
    groups = count_dp // group
    near = min(4, count_dp)
    far = count_dp // near
    vmem = pl.BlockSpec(memory_space=pltpu.VMEM)
    hbm = pl.BlockSpec(memory_space=pl.ANY)
    sem = pltpu.SemaphoreType.DMA
    in_sums, products, x_all, g_all, act, pre_grad = pl.pallas_call(
        functools.partial(exchange_kernel, count_dp, near),
        out_shape=(
            jax.ShapeDtypeStruct((rows, feats), F32),
            jax.ShapeDtypeStruct((tokens, width), F32),
            jax.ShapeDtypeStruct((tokens, feats), BF16),
            jax.ShapeDtypeStruct((tokens, feats), BF16),
            jax.ShapeDtypeStruct((tokens, width), BF16),
            jax.ShapeDtypeStruct((tokens, width), BF16),
        ),
        in_specs=[vmem, hbm, hbm],
        out_specs=(vmem,) * 6,
        scratch_shapes=[
            pltpu.VMEM((feats, width), BF16),
            pltpu.VMEM((width, feats), BF16),
            pltpu.VMEM((2, count_dp, 2, TILE, lanes), BF16),
            pltpu.VMEM((2, group * TILE, group * TILE), BF16),
            pltpu.VMEM((2, groups, group * TILE, lanes), BF16),
            pltpu.VMEM((count_dp, TILE, lanes), BF16),
            pltpu.VMEM((count_dp, TILE, lanes), BF16),
            pltpu.VMEM((count_dp, TILE, lanes), F32),
            pltpu.VMEM((count_dp, TILE, lanes), BF16),
            pltpu.VMEM((far, near - 1, TILE, lanes), BF16),
            pltpu.VMEM((far - 1, TILE, lanes), BF16),
            pltpu.VMEM((far - 1, TILE, lanes), BF16),
            sem((8,)),
            sem((far - 1,)), sem((far - 1,)),
            sem((far, near - 1)), sem((far, near - 1)),
            sem((far, near)), sem((far, near)),
            sem((far,)), sem((far,)),
            sem((far, near - 1)), sem((far, near - 1)),
            sem((far - 1,)), sem((far - 1,)),
        ],
        compiler_params=pltpu.CompilerParams(
            collective_id=0, has_side_effects=True, vmem_limit_bytes=48 * 2**20
        ),
        cost_estimate=pl.CostEstimate(
            flops=6 * tokens * feats * width, bytes_accessed=4 * feats * width, transcendentals=0
        ),
        name="exchange",
    )(jnp.concatenate([inputs, out_grad], axis=0), up_weight, down_weight)
    parts = 8
    fixed = lambda i: (0, 0)
    return pl.pallas_call(
        functools.partial(weight_grads_kernel, count_dp),
        grid=(parts,),
        out_shape=(
            jax.ShapeDtypeStruct((rows, feats), BF16),
            jax.ShapeDtypeStruct((NBLK, width), F32),
            jax.ShapeDtypeStruct((feats, width), BF16),
            jax.ShapeDtypeStruct((width, feats), BF16),
        ),
        in_specs=[
            pl.BlockSpec((rows, feats), fixed),
            pl.BlockSpec((tokens, width), fixed),
            pl.BlockSpec((1, tokens), fixed),
            pl.BlockSpec((tokens, feats // parts), lambda i: (0, i)),
            pl.BlockSpec((tokens, width), fixed),
            pl.BlockSpec((tokens, width), fixed),
            pl.BlockSpec((tokens, feats // parts), lambda i: (0, i)),
        ],
        out_specs=(
            pl.BlockSpec((rows, feats), fixed),
            pl.BlockSpec((NBLK, width), fixed),
            pl.BlockSpec((feats // parts, width), lambda i: (i, 0)),
            pl.BlockSpec((width, feats // parts), lambda i: (0, i)),
        ),
        compiler_params=pltpu.CompilerParams(vmem_limit_bytes=32 * 2**20),
        cost_estimate=pl.CostEstimate(
            flops=4 * tokens * feats * width, bytes_accessed=4 * feats * width, transcendentals=0
        ),
        name="weight_grads",
    )(in_sums, products, block_ids.reshape(1, tokens), x_all, pre_grad, act, g_all)


def solution(mesh):
    return jax.shard_map(
        on_device,
        mesh=mesh,
        in_specs=(
            P(("groups", "dp", "tensor"), None),
            P(("groups", "dp", "tensor"), None),
            P("groups"),
            P(None, ("dp", "tensor")),
            P(("dp", "tensor"), None),
        ),
        out_specs=(
            P(("groups", "dp", "tensor"), None),
            P("groups", ("dp", "tensor")),
            P("groups", ("dp", "tensor")),
            P(("groups", "dp", "tensor"), None),
        ),
        check_vma=False,
    )
```

time: 56 us -> 42.7 us (0.76)
  Pallas kernels: 51.7 us -> 40.9 us
  local copies, waits for them, and re-layouts: 3.32 us -> 0.01 us
  other arithmetic: 0 us -> 0.77 us
    pallas_call x2, Pallas kernels: 51.7 us -> 40.9 us  [the longest x1 32.7 us: on_device(): pl.pallas_call(functools.partial(exchange_kernel, count_dp, near), out_sh...]
    unnamed x8 -> x2, local copies, waits for them, and re-layouts: 3.32 us -> 0.01 us
    concatenate x0 -> x1, other arithmetic: none -> 0.77 us  [on_device(): jnp.concatenate([inputs, out_grad], axis=0)]
where the time goes in v2:
time: 42.7 us; the launch traced here: 42.4 us
  Pallas kernels  40.9 us (96%)
  other arithmetic  0.77 us (2%)
  between operations  0.66 us (2%)
    pallas_call x1, Pallas kernels, on_device(): pl.pallas_call(functools.partial(exchange_kernel, count_dp, near), out_sh...  32.7 us
    pallas_call x1, Pallas kernels, on_device(): pl.pallas_call(functools.partial(weight_grads_kernel, count_dp), grid=(pa...  8.22 us

profile of v2, /device:TPU:0, one launch (start us, length us, event | category | flops | bytes accessed | tf_op | source)
XLA Modules:
  0.0 42.4 jit_solution(908539503900629458)
XLA Ops:
  0.6 0.8 %pad_maximum_fusion.xg_ref = bf16[4,4096]{1,0:T(4,128)(2,1)S(1)} fusion(bf16[2,4096]{1,0:T(2,128)(2,1)} %param.6, bf16[2,4096]{1,0:T(2,128)(2,1)} %param.5), kind=kLoop, calls=%fused_computation | loop fusion | flops 65536 | bytes 65536 | tf_op jit(solution)/shard_map/concatenate | solution.py:271
  1.4 0.0 copy-start
  1.4 32.7 %exchange.1 = (f32[2,4096]{1,0:T(2,128)S(1)}, f32[64,1024]{1,0:T(8,128)S(1)}, bf16[64,4096]{1,0:T(8,128)(2,1)S(1)}, bf16[64,4096]{1,0:T(8,128)(2,1)S(1)}, bf16[6...) custom-call(bf16[4,4096]{1,0:T(4,128)(2,1)S(1)} %pad_maximum_fusion.xg_ref, bf16[4096,1024]{1,0:T(8,128)(2,1)} %up_hbm.1, ...), custom_call_target="tpu_custom_call" | custom-call | flops 1610612736 | bytes 16777216 | tf_op jit(solution)/shard_map/exchange/pallas_call | solution.py:231
  34.1 0.0 copy-done
  34.1 8.2 %weight_grads.1 = (bf16[2,4096]{1,0:T(2,128)(2,1)}, f32[16,1024]{1,0:T(8,128)}, bf16[4096,1024]{1,0:T(8,128)(2,1)}, bf16[1024,4096]{1,0:T(8,128)(2,1)}) custom-call(f32[2,4096]{1,0:T(2,128)S(1)} %get-tuple-element.10.sum_ref, f32[64,1024]{1,0:T(8,128)S(1)} %get-tuple-element.11.prod_ref, s32[1,64]{1,0:T(1,128)S(1)} %bitcast.1, ...), custom_call_target="tpu_custom_call" | custom-call | flops 1073741824 | bytes 16777216 | tf_op jit(solution)/shard_map/weight_grads/pallas_call | solution.py:274
Async XLA Ops:
  1.4 32.7 %copy-start = (s32[64]{0:T(128)S(1)}, s32[64]{0:T(128)}, u32[]{:S(2)}) copy-start(s32[64]{0:T(128)} %param.7) | copy-start | bytes 772

commit v3 on v2

--- a/solution.py
+++ b/solution.py
@@ -269,7 +269,8 @@
         ),
         name="exchange",
     )(jnp.concatenate([inputs, out_grad], axis=0), up_weight, down_weight)
-    parts = 8
+    parts = 4
+    act_parts = min(parts, width // 128)
     fixed = lambda i: (0, 0)
     return pl.pallas_call(
         functools.partial(weight_grads_kernel, count_dp),
@@ -286,14 +287,14 @@
             pl.BlockSpec((1, tokens), fixed),
             pl.BlockSpec((tokens, feats // parts), lambda i: (0, i)),
             pl.BlockSpec((tokens, width), fixed),
-            pl.BlockSpec((tokens, width), fixed),
-            pl.BlockSpec((tokens, feats // parts), lambda i: (0, i)),
+            pl.BlockSpec((tokens, width // act_parts), lambda i: (0, i * act_parts // parts)),
+            pl.BlockSpec((tokens, feats * act_parts // parts), lambda i: (0, i % (parts // act_parts))),
         ],
         out_specs=(
             pl.BlockSpec((rows, feats), fixed),
             pl.BlockSpec((NBLK, width), fixed),
             pl.BlockSpec((feats // parts, width), lambda i: (i, 0)),
-            pl.BlockSpec((width, feats // parts), lambda i: (0, i)),
+            pl.BlockSpec((width // act_parts, feats * act_parts // parts), lambda i: (i * act_parts // parts, i % (parts // act_parts))),
         ),
         compiler_params=pltpu.CompilerParams(vmem_limit_bytes=32 * 2**20),
         cost_estimate=pl.CostEstimate(

time: 42.7 us -> 41.8 us (0.979)
  Pallas kernels: 40.9 us -> 40 us
    pallas_call x1, Pallas kernels: 8.22 us -> 7.27 us  [on_device(): pl.pallas_call(functools.partial(weight_grads_kernel, count_dp), grid=(pa...]
where the time goes in v3:
time: 41.8 us; the launch traced here: 41.4 us
  Pallas kernels  40 us (96%)
  other arithmetic  0.77 us (2%)
  between operations  0.66 us (2%)
    pallas_call x1, Pallas kernels, on_device(): pl.pallas_call(functools.partial(exchange_kernel, count_dp, near), out_sh...  32.7 us
    pallas_call x1, Pallas kernels, on_device(): pl.pallas_call(functools.partial(weight_grads_kernel, count_dp), grid=(pa...  7.27 us

profile of v3, /device:TPU:0, one launch (start us, length us, event | category | flops | bytes accessed | tf_op | source)
XLA Modules:
  0.0 41.4 jit_solution(2245842091436610957)
XLA Ops:
  0.6 0.8 %pad_maximum_fusion.xg_ref = bf16[4,4096]{1,0:T(4,128)(2,1)S(1)} fusion(bf16[2,4096]{1,0:T(2,128)(2,1)} %param.6, bf16[2,4096]{1,0:T(2,128)(2,1)} %param.5), kind=kLoop, calls=%fused_computation | loop fusion | flops 65536 | bytes 65536 | tf_op jit(solution)/shard_map/concatenate | solution.py:271
  1.4 0.0 copy-start
  1.4 32.7 %exchange.1 = (f32[2,4096]{1,0:T(2,128)S(1)}, f32[64,1024]{1,0:T(8,128)S(1)}, bf16[64,4096]{1,0:T(8,128)(2,1)S(1)}, bf16[64,4096]{1,0:T(8,128)(2,1)S(1)}, bf16[6...) custom-call(bf16[4,4096]{1,0:T(4,128)(2,1)S(1)} %pad_maximum_fusion.xg_ref, bf16[4096,1024]{1,0:T(8,128)(2,1)} %up_hbm.1, ...), custom_call_target="tpu_custom_call" | custom-call | flops 1610612736 | bytes 16777216 | tf_op jit(solution)/shard_map/exchange/pallas_call | solution.py:231
  34.1 0.0 copy-done
  34.1 7.3 %weight_grads.1 = (bf16[2,4096]{1,0:T(2,128)(2,1)}, f32[16,1024]{1,0:T(8,128)}, bf16[4096,1024]{1,0:T(8,128)(2,1)}, bf16[1024,4096]{1,0:T(8,128)(2,1)}) custom-call(f32[2,4096]{1,0:T(2,128)S(1)} %get-tuple-element.10.sum_ref, f32[64,1024]{1,0:T(8,128)S(1)} %get-tuple-element.11.prod_ref, s32[1,64]{1,0:T(1,128)S(1)} %bitcast.1, ...), custom_call_target="tpu_custom_call" | custom-call | flops 1073741824 | bytes 16777216 | tf_op jit(solution)/shard_map/weight_grads/pallas_call | solution.py:275
Async XLA Ops:
  1.4 32.7 %copy-start = (s32[64]{0:T(128)S(1)}, s32[64]{0:T(128)}, u32[]{:S(2)}) copy-start(s32[64]{0:T(128)} %param.7) | copy-start | bytes 772
